TPU v7x, 256 devices: a whole 4x4x8 slice. The times are simulated.
256 devices in a mesh: row: 32 (over y, x, core), col: 8 (over z).
Axes of the slice: x: 4, y: 4, z: 8, core: 2. Of those that a mesh axis runs over, the one named last changes fastest.
Arguments:
- panel: float32 [4, 4096, 256], P(None, 'row'), may hold values from -1.5 to 1.5, as said below
- matrix: float32 [4, 4096, 16, 1024], P(None, 'row', None, 'col'), may hold values from -40 to 40, as said below
Outputs:
- factor: float32 [256, 256], replicated
- updated: float32 [4, 4096, 16, 1024], P(None, 'row', None, 'col')
Inputs may be any that keep to these rules, and one draw needn't show every extreme that they name: matrix, read as an 16384 x 16384 matrix, is exactly symmetric. panel has full column rank.
All inputs are finite; a program needn't handle non-finite values.
Results may differ from a plain program's by a relative error of at most 0.000061.
Values sent between devices are 32-bit elements; how exact they have to be, the bound alone decides.
A program may use at most 64 MiB of HBM per device.

v0:
```python
import jax
import jax.numpy as jnp
from jax import lax
from jax.sharding import PartitionSpec as P


def shards(panel, matrix):
    highest = lax.Precision.HIGHEST
    row_count = lax.axis_size("row")
    col_count = lax.axis_size("col")
    ratio = row_count // col_count
    row_place = lax.axis_index("row")
    col_place = lax.axis_index("col")
    row_cycles, block_rows, width = panel.shape
    col_cycles = matrix.shape[2]
    rows = panel.reshape(row_cycles * block_rows, width)
    local = matrix.reshape(row_cycles * block_rows, col_cycles * block_rows)
    owner = row_place % col_count == col_place
    slots = (jnp.arange(ratio) == row_place // col_count) & owner
    spread_mask = slots.astype(jnp.float32)[None, :, None, None]
    gram = lax.psum(jnp.dot(rows.T, rows, precision=highest), "row")
    lower = jnp.linalg.cholesky(gram)
    across = lax.psum(panel[:, None] * spread_mask, "row")
    col_rows = across.reshape(col_cycles * block_rows, width)

    def orthonormal(values):
        return jax.scipy.linalg.solve_triangular(lower, values.T, lower=True).T

    basis = orthonormal(rows)
    col_basis = orthonormal(col_rows)
    partial_image = jnp.dot(local, col_basis, precision=highest)
    image = lax.psum(partial_image, "col")
    curvature = lax.psum(jnp.dot(basis.T, image, precision=highest), "row")
    wing = 2.0 * image - 2.0 * jnp.dot(basis, curvature, precision=highest)
    shaped = wing.reshape(row_cycles, block_rows, width)[:, None] * spread_mask
    col_wing = lax.psum(shaped, "row").reshape(col_cycles * block_rows, width)
    left_side = jnp.concatenate([basis, wing], axis=1)
    right_side = jnp.concatenate([col_wing, col_basis], axis=1)
    result = local - jnp.dot(left_side, right_side.T, precision=highest)
    return (lower.T, result.reshape(matrix.shape))


def solution(mesh):
    in_specs = (P(None, "row", None), P(None, "row", None, "col"))
    out_specs = (P(), P(None, "row", None, "col"))
    return jax.shard_map(shards, mesh=mesh, in_specs=in_specs, out_specs=out_specs, check_vma=False)
```

profile of v0, /device:TPU:1, one launch (start us, length us, event | category | flops | bytes accessed | tf_op | source)
XLA Modules:
  0.0 539.8 jit_solution(11284084831781511993)
XLA Ops:
  7.2 0.0 all-reduce.13.cloned.1.call-start
  7.2 2.9 convolution_bitcast_fusion
  10.2 1.3 copy.7
  11.5 0.4 broadcast_multiply_fusion.1
  11.9 1.8 reshape.54
  13.7 0.0 all-reduce.13.cloned.1.call-update
  13.8 0.0 all-reduce.7.cloned.1.call-start
  13.8 121.5 %all-reduce.13.cloned.1.call-done = (f32[256,256]{0,1:T(8,128)}, f32[256,2048]{1,0:T(8,128)}) async-done(((f32[256,256]{0,1:T(8,128)}, f32[256,2048]{1,0:T(8,128)}), (f32[256,256]{0,1:T(8,128)}, f32[256,2048]{1,0:T(8,128)})) %all-reduce.13.cloned.1.call-update) | async-done | bytes 2359312 | tf_op jit(solution)/shard_map/psum | solution.py:21
  135.4 1.2 copy.6
  136.6 1.0 fusion.24
  137.6 11.7 %cholesky.50 = f32[128,128]{1,0:T(8,128)S(1)} custom-call(f32[128,128]{1,0:T(8,128)S(1)} %cholesky.118), custom_call_target="Cholesky" | custom-call | tf_op jit(solution)/shard_map/jit(cholesky)/cholesky | solution.py:22
  149.3 9.8 %custom-call.18 = f32[1,128,128]{1,2,0:T(8,128)S(1)} custom-call(f32[1,128,128]{2,1,0:T(8,128)S(1)} %get-tuple-element.29), custom_call_target="InvertDiagBlocksLowerTriangular" | custom-call | tf_op jit(solution)/shard_map/jit(cholesky)/cholesky | solution.py:22
  159.2 0.2 constant_dynamic-update-slice_fusion.1
  159.4 0.3 convolution_subtract_fusion.2
  159.7 11.7 %cholesky.105 = f32[128,128]{1,0:T(8,128)S(1)} custom-call(f32[128,128]{1,0:T(8,128)S(1)} %convolution_subtract_fusion.2), custom_call_target="Cholesky" | custom-call | tf_op jit(solution)/shard_map/jit(cholesky)/cholesky | solution.py:22
  171.4 0.6 compare_reduce_fusion
  173.4 0.7 fusion.25
  174.1 0.1 triangular_solve.57
  174.2 3.8 while.1
  174.2 0.6 fusion.50
  174.8 1.3 bitcast_dynamic-update-slice_fusion.2
  176.1 0.6 fusion.50
  176.7 1.3 bitcast_dynamic-update-slice_fusion.2
  178.0 19.7 %custom-call.19 = f32[2,128,128]{1,2,0:T(8,128)S(1)} custom-call(f32[2,128,128]{2,1,0:T(8,128)S(1)} %get-tuple-element.9), custom_call_target="InvertDiagBlocksLowerTriangular" | custom-call | tf_op jit(solution)/shard_map/jit(_solve_triangular)/triangular_solve | solution.py:27
  197.7 1.1 fusion.15
  198.7 1.0 convolution_subtract_fusion
  199.8 1.0 fusion.30
  200.8 0.1 copy-done
  200.9 5.7 %fusion.11 = f32[512,256]{0,1:T(8,128)} fusion(f32[64,8,16,128]{3,2,1,0:T(8,128)S(1)} %bitcast.74, f32[128,2048]{1,0:T(8,128)S(1)} %fusion.30, f32[128,2048]{1,0:T(8,128)S(1)} %fusion.15), kind=kOutput, calls=%fused_computation.14 | convolution fusion | flops 3221749760 | bytes 6815744 | tf_op jit(solution)/shard_map/dot_general | solution.py:31
  206.7 0.3 all-reduce.9.cloned.1.call-start
  207.0 0.4 fusion.22
  207.4 0.6 convolution_subtract_fusion.1
  208.0 0.4 fusion.31
  208.4 67.1 %all-reduce.7.cloned.1.call-done = f32[512,256]{0,1:T(8,128)} async-done(((f32[512,256]{0,1:T(8,128)}), f32[512,256]{0,1:T(8,128)}) %all-reduce.7.cloned.1.call-update) | async-done | bytes 524304 | tf_op jit(solution)/shard_map/psum | solution.py:32
  275.5 2.4 fusion.20
  277.9 0.0 all-reduce.11.cloned.1.call-start
  278.0 116.1 %all-reduce.9.cloned.1.call-done = f32[256,256]{1,0:T(8,128)} async-done(((f32[256,256]{1,0:T(8,128)}), f32[256,256]{1,0:T(8,128)}) %all-reduce.9.cloned.1.call-update) | async-done | bytes 262160 | tf_op jit(solution)/shard_map/psum | solution.py:33
  394.0 1.8 fusion.14
  395.9 1.0 mul.37
  396.8 2.8 broadcast_multiply_fusion
  399.6 3.0 reshape.55
  402.7 0.9 copy-done.4
  403.6 0.8 copy.9
  404.4 0.8 fusion.21
  405.3 1.5 fusion.10
  406.7 113.3 %all-reduce.11.cloned.1.call-done = f32[2048,256]{0,1:T(8,128)} async-done(((f32[2048,256]{0,1:T(8,128)}), f32[2048,256]{0,1:T(8,128)}) %all-reduce.11.cloned.1.call-update) | async-done | bytes 2097168 | tf_op jit(solution)/shard_map/psum | solution.py:36
  520.1 10.3 %fusion.2 = f32[64,8,16,128]{3,1,2,0:T(8,128)S(1)} fusion(f32[64,8,16,128]{3,2,1,0:T(8,128)} %bitcast.73, f32[2048,256]{0,1:T(8,128)} %fusion.10, f32[2048,256]{0,1:T(8,128)} %all-reduce.11.cloned.1.call-done, f32[512,256]{0,1:T(8,128)S(1)} %fusion.14, f32[512,256]{0,1:T(8,128)S(1)} %copy-done.3), kind=kOutput, calls=%fused_computation.5 | convolution fusion | flops 6444810240 | bytes 13631488 | tf_op jit(solution)/shard_map/dot_general | solution.py:39
  530.4 2.9 copy.15
  (20 shorter events, 0.2 us)
Async XLA Ops:
  7.2 128.2 %all-reduce.13.cloned.1.call-start = ((), (), s32[]{:S(2)}) async-start(), calls=%async_computation.3 | async-start | bytes 4718592 | tf_op jit(solution)/shard_map/psum | solution.py:21
  13.8 261.8 %all-reduce.7.cloned.1.call-start = ((), (), s32[]{:S(2)}) async-start(), calls=%async_computation | async-start | bytes 1048576 | tf_op jit(solution)/shard_map/psum | solution.py:32
  135.4 62.3 %copy-start.2 = (f32[256,2048]{1,0:T(8,128)S(1)}, f32[256,2048]{1,0:T(8,128)}, u32[]{:S(2)}) copy-start(f32[256,2048]{1,0:T(8,128)} %get-tuple-element.21) | copy-start | bytes 6291460
  198.7 2.2 copy-start
  200.9 6.0 %copy-start.1 = (f32[4,128,256]{2,1,0:T(8,128)S(1)}, f32[4,128,256]{2,1,0:T(8,128)}, u32[]{:S(2)}) copy-start(f32[4,128,256]{2,1,0:T(8,128)} %param.2) | copy-start | bytes 1572868
  206.7 187.4 %all-reduce.9.cloned.1.call-start = ((), (), s32[]{:S(2)}) async-start(), calls=%async_computation.1 | async-start | bytes 524288 | tf_op jit(solution)/shard_map/psum | solution.py:33
  277.9 242.1 %all-reduce.11.cloned.1.call-start = ((), (), s32[]{:S(2)}) async-start(), calls=%async_computation.2 | async-start | bytes 4194304 | tf_op jit(solution)/shard_map/psum | solution.py:36
  402.6 0.9 copy-start.4
  405.3 114.8 %copy-start.3 = (f32[512,256]{0,1:T(8,128)S(1)}, f32[512,256]{0,1:T(8,128)}, u32[]{:S(2)}) copy-start(f32[512,256]{0,1:T(8,128)} %fusion.21) | copy-start | bytes 1572868
Sparse Core Ops, SparseCore 0:
  13.9 121.4 all-reduce.12
  206.8 68.6 all-reduce.6
  279.7 114.3 all-reduce.8
  402.8 117.2 all-reduce.10
where the time goes:
time: 540 us
  waiting for transfers between devices  418 us (77%)
  other arithmetic  60.9 us (11%)
  matrix products  28.2 us (5%)
  local copies, waits for them, and re-layouts  17 us (3%)
  between operations  15.3 us (3%)
    psum x1, waiting for transfers between devices, shards(): gram = lax.psum(jnp.dot(rows.T, rows, precision=highest), 'row')  122 us
    psum x1, waiting for transfers between devices, shards(): curvature = lax.psum(jnp.dot(basis.T, image, precision=highest), 'row')  116 us
    psum x1, waiting for transfers between devices, shards(): col_wing = lax.psum(shaped, 'row').reshape(col_cycles * block_rows, width)  113 us
    psum x1, waiting for transfers between devices, shards(): image = lax.psum(partial_image, 'col')  67.1 us
    another operation x6, other arithmetic, shards(): lower = jnp.linalg.cholesky(gram)  34 us
    another operation x3, other arithmetic, orthonormal(): return jax.scipy.linalg.solve_triangular(lower, values.T, lower=True).T  20.4 us
  transfers between devices with their start and end apart: 4, of which 4 were waited for; matrix products, arithmetic and copies ran while one was open for 1% of the time, Pallas kernels for 0%

commit v1 on v0

v1 whole, which is shorter than its diff:
```python
import functools

import jax
import jax.numpy as jnp
from jax import lax
from jax.experimental import pallas as pl
from jax.experimental.pallas import tpu as pltpu
from jax.sharding import PartitionSpec as P

MESH = pl.DeviceIdType.MESH
HIGHEST = lax.Precision.HIGHEST
F32 = jnp.float32
BF16 = jnp.bfloat16
W = 256
ROWS = 512
CHUNK = 64
NCH = 4
NB = 32


def remote(src, dst, send, recv, row, col):
    return pltpu.make_async_remote_copy(
        src_ref=src, dst_ref=dst, send_sem=send, recv_sem=recv,
        device_id={"row": row, "col": col}, device_id_type=MESH)


def split(x):
    hi = x.astype(BF16)
    return hi, (x - hi.astype(F32)).astype(BF16)


NN = (((1,), (0,)), ((), ()))
NT = (((1,), (1,)), ((), ()))
TN = (((0,), (0,)), ((), ()))


def dot(a, b, dims=NN, precision=None):
    return lax.dot_general(a, b, dims, precision=precision, preferred_element_type=F32)


def dot3(a, b, dims=NN):
    ah, al = split(a)
    bh, bl = split(b)
    return dot(ah, bh, dims) + (dot(ah, bl, dims) + dot(al, bh, dims))


def factorize(gram, work):
    lane = lax.broadcasted_iota(jnp.int32, (NB, 128), 1)
    sub = lax.broadcasted_iota(jnp.int32, (NB, 128), 0)
    eye = (lane == sub).astype(F32)
    for b in range(W // NB):
        lo = b * NB
        left = gram[lo:lo + NB, :]
        unit = (lax.broadcasted_iota(jnp.int32, (NB, W), 1) ==
                lax.broadcasted_iota(jnp.int32, (NB, W), 0) + lo).astype(F32)
        rows = jnp.concatenate([left, unit], axis=1)
        if b:
            rows = rows - dot(work[0:lo, lo:lo + NB], work[0:lo, :], TN, HIGHEST)
        tile = jnp.concatenate([rows[:, lo:lo + NB], eye[:, :NB], jnp.zeros((NB, 128 - 2 * NB), F32)], axis=1)
        for i in range(NB):
            row = tile[i:i + 1, :]
            factor = tile[:, i:i + 1] * (1.0 / tile[i:i + 1, i:i + 1])
            tile = jnp.where(sub > i, tile - factor * row, tile)
        pivots = jnp.sum(jnp.where(lane == sub, tile, 0.0), axis=1, keepdims=True)
        inverse = tile[:, NB:2 * NB] * lax.rsqrt(pivots)
        work[lo:lo + NB, :] = dot(inverse, rows, NN, HIGHEST)


def body(panel, a_hbm, factor_out, out_hbm,
         abuf, ahi, alo, pc, yc, chi, clo, part, yrow, rsbuf, gpart, gsum, grs, spart, ssum, srs, work, lhs,
         a_sem, o_sem, px, py, ps, p0, yx, yy, ys, y0, gr, ga, gs, sr, sa, ss, rr, ra):
    r = lax.axis_index("row")
    c = lax.axis_index("col")
    core = r % 2
    x = (r // 2) % 4
    y = r // 8
    sib = r + 1 - 2 * core
    step = 1 + 2 * core

    def at_row(xx, yy_):
        return (yy_ * 4 + xx) * 2 + core

    xdst = at_row((x + step) % 4, y)
    ydst = at_row(x, (y + step) % 4)
    source_x = c // 2
    source_core = c % 2
    hop = ((x + 4 - source_x) * step) % 4

    load = pltpu.make_async_copy(a_hbm, abuf, a_sem)
    load.start()

    barrier = pltpu.get_barrier_semaphore()
    for row in (sib, at_row((x + 1) % 4, y), at_row((x + 3) % 4, y), at_row(x, (y + 1) % 4), at_row(x, (y + 3) % 4)):
        pl.semaphore_signal(barrier, inc=1, device_id={"row": row, "col": c}, device_id_type=MESH)
    for p in range(1, 8):
        pl.semaphore_signal(barrier, inc=1, device_id={"row": r, "col": (c + p) % 8}, device_id_type=MESH)
    pl.semaphore_wait(barrier, 12)

    on_source = hop == 0
    is_source = jnp.logical_and(on_source, core == source_core)
    is_second = jnp.logical_and(on_source, core != source_core)

    def gather(src, buf, sx, sy, ss_, s0):
        def piece(q, half, t):
            return buf.at[q, pl.ds(half * (NCH * CHUNK) + t * CHUNK, CHUNK), :]

        @pl.when(is_source)
        def _():
            buf[y] = src[...]
            for t in range(NCH):
                ref = piece(y, 1 - core, t)
                remote(ref, ref, s0.at[0, t], s0.at[1, t], sib, c).start()

        for t in range(NCH):
            ref = piece(y, core, t)
            first = remote(ref, ref, s0.at[0, t], s0.at[1, t], sib, c)
            along = remote(ref, ref, sx.at[0, t], sx.at[1, t], xdst, c)

            @pl.when(is_second)
            def _():
                first.wait_recv()

            @pl.when(hop > 0)
            def _():
                along.wait_recv()

            @pl.when(hop < 3)
            def _():
                along.start()

            remote(ref, ref, sy.at[0, 0, t], sy.at[1, 0, t], ydst, c).start()

            @pl.when(jnp.logical_not(is_second))
            def _():
                remote(ref, ref, ss_.at[0, 0, t], ss_.at[1, 0, t], sib, c).start()

        for s in range(1, 4):
            q = (y + 4 * step - s * step) % 4
            for t in range(NCH):
                ref = piece(q, core, t)
                remote(ref, ref, sy.at[0, s - 1, t], sy.at[1, s - 1, t], ydst, c).wait_recv()
                if s < 3:
                    remote(ref, ref, sy.at[0, s, t], sy.at[1, s, t], ydst, c).start()
                remote(ref, ref, ss_.at[0, s, t], ss_.at[1, s, t], sib, c).start()
        for s in range(4):
            q = (y + s * step) % 4
            for t in range(NCH):
                other = piece(q, 1 - core, t)
                copy = remote(other, other, ss_.at[0, s, t], ss_.at[1, s, t], sib, c)
                if s:
                    copy.wait_recv()
                else:
                    @pl.when(jnp.logical_not(is_source))
                    def _():
                        copy.wait_recv()
        for t in range(NCH):
            ref = piece(y, core, t)

            @pl.when(is_source)
            def _():
                remote(ref, ref, s0.at[0, t], s0.at[1, t], sib, c).wait_send()

            @pl.when(hop < 3)
            def _():
                remote(ref, ref, sx.at[0, t], sx.at[1, t], xdst, c).wait_send()

            for s in range(3):
                remote(ref, ref, sy.at[0, s, t], sy.at[1, s, t], ydst, c).wait_send()
            for s in range(4):
                copy = remote(ref, ref, ss_.at[0, s, t], ss_.at[1, s, t], sib, c)
                if s:
                    copy.wait_send()
                else:
                    @pl.when(jnp.logical_not(is_second))
                    def _():
                        copy.wait_send()

    def scatter_copy(src, dst, sems, rows, p):
        z = (c + p) % 8
        return remote(src.at[pl.ds(z * rows, rows), :], dst.at[p], sems.at[0, p], sems.at[1, p], r, z)

    def spread_copy(ref, base, sems, rows, p):
        z = (c + p) % 8
        piece = ref.at[pl.ds(base + c * rows, rows), :]
        return remote(piece, piece, sems.at[0, p], sems.at[1, p], r, z)

    def spread_wait(ref, base, sems, rows, p):
        z = (c + 8 - p) % 8
        piece = ref.at[pl.ds(base + z * rows, rows), :]
        remote(piece, piece, sems.at[0, p], sems.at[1, p], r, (c + p) % 8).wait_recv()

    def reduce_small(partial, slots, total, s_scatter, s_spread, s_sib):
        for p in range(1, 8):
            scatter_copy(partial, slots, s_scatter, 16, p).start()
        for p in range(1, 8):
            scatter_copy(partial, slots, s_scatter, 16, p).wait_recv()
        value = partial[pl.ds(pl.multiple_of(c * 16, 16), 16), :]
        for p in range(1, 8):
            value = value + slots[p]
        base = core * 128
        total[pl.ds(pl.multiple_of(base + c * 16, 16), 16), :] = value
        for p in range(1, 8):
            spread_copy(total, base, s_spread, 16, p).start()
        for p in range(1, 8):
            spread_wait(total, base, s_spread, 16, p)
        half = total.at[pl.ds(base, 128), :]
        other = total.at[pl.ds(128 - base, 128), :]
        share = remote(half, half, s_sib.at[0], s_sib.at[1], sib, c)
        share.start()
        remote(other, other, s_sib.at[0], s_sib.at[1], sib, c).wait_recv()
        for p in range(1, 8):
            scatter_copy(partial, slots, s_scatter, 16, p).wait_send()
            spread_copy(total, base, s_spread, 16, p).wait_send()
        share.wait_send()

    gather(panel, pc, px, py, ps, p0)

    mine = pl.ds(pl.multiple_of(core * 128, 128), 128)
    gpart[...] = jnp.zeros_like(gpart)

    @pl.loop(0, 4)
    def _(q):
        gpart[...] += dot(pc[q, :, mine], pc[q], TN, HIGHEST)

    reduce_small(gpart, grs, gsum, gr, ga, gs)

    load.wait()
    part[...] = jnp.zeros_like(part)
    for q in range(4):
        for i in range(4):
            h, l = split(abuf[pl.ds(4 * i + q, ROWS, stride=16), :])
            ahi[q, :, i * 128:(i + 1) * 128] = h
            alo[q, :, i * 128:(i + 1) * 128] = l

    @pl.loop(0, 4)
    def _(q):
        h, l = split(pc[q])
        chi[q, :, W:] = h
        clo[q, :, W:] = l
        part[...] += dot(ahi[q], h) + (dot(ahi[q], l) + dot(alo[q], h))

    for p in range(1, 8):
        scatter_copy(part, rsbuf, rr, 64, p).start()
    factorize(gsum, work)
    upper = lax.broadcasted_iota(jnp.int32, (W, W), 1) >= lax.broadcasted_iota(jnp.int32, (W, W), 0)
    factor_out[...] = jnp.where(upper, work[:, :W], 0.0)
    inverse = work[:, W:]
    metric = dot(inverse, inverse, TN, HIGHEST)
    first = 2.0 * dot3(panel[...], metric)
    for p in range(1, 8):
        scatter_copy(part, rsbuf, rr, 64, p).wait_recv()
    own = pl.ds(pl.multiple_of(c * 64, 64), 64)
    value = part[own, :]
    for p in range(1, 8):
        value = value + rsbuf[p]
    yrow[own, :] = value
    for p in range(1, 8):
        spread_copy(yrow, 0, ra, 64, p).start()
    for p in range(1, 8):
        spread_wait(yrow, 0, ra, 64, p)

    gather(yrow, yc, yx, yy, ys, y0)

    spart[...] = jnp.zeros_like(spart)

    @pl.loop(0, 4)
    def _(q):
        h, l = split(yc[q])
        chi[q, :, :W] = h
        clo[q, :, :W] = l
        spart[...] += dot3(pc[q, :, mine], yc[q], TN)

    reduce_small(spart, srs, ssum, sr, sa, ss)

    second = 2.0 * dot3(yrow[...] - dot3(first, ssum[...]), metric)
    lhs[0, :, :W], lhs[1, :, :W] = split(first)
    lhs[0, :, W:], lhs[1, :, W:] = split(second)

    @pl.loop(0, 4)
    def _(m):
        rows = pl.ds(pl.multiple_of(m * 128, 128), 128)
        lh = lhs[0, rows, :]
        ll = lhs[1, rows, :]
        for q in range(4):
            value = dot(lh, chi[q], NT) + (dot(lh, clo[q], NT) + dot(ll, chi[q], NT))
            for i in range(4):
                at = pl.ds(m * 2048 + 4 * i + q, 128, stride=16)
                abuf[at, :] = abuf[at, :] - value[:, i * 128:(i + 1) * 128]
        block = pl.ds(pl.multiple_of(m * 2048, 2048), 2048)
        pltpu.make_async_copy(abuf.at[block, :], out_hbm.at[block, :], o_sem.at[m]).start()

    for p in range(1, 8):
        scatter_copy(part, rsbuf, rr, 64, p).wait_send()
        spread_copy(yrow, 0, ra, 64, p).wait_send()
    for m in range(4):
        block = pl.ds(m * 2048, 2048)
        pltpu.make_async_copy(abuf.at[block, :], out_hbm.at[block, :], o_sem.at[m]).wait()


def shards(panel, matrix):
    vmem = functools.partial(pltpu.VMEM)
    dma = pltpu.SemaphoreType.DMA
    gather_sems = [dma((2, NCH)), dma((2, 3, NCH)), dma((2, 4, NCH)), dma((2, NCH))]
    small_sems = [dma((2, 8)), dma((2, 8)), dma((2,))]
    factor, updated = pl.pallas_call(
        body,
        out_shape=(jax.ShapeDtypeStruct((W, W), F32), jax.ShapeDtypeStruct((ROWS * 16, 128), F32)),
        in_specs=[pl.BlockSpec(memory_space=pltpu.VMEM), pl.BlockSpec(memory_space=pl.ANY)],
        out_specs=(pl.BlockSpec(memory_space=pltpu.VMEM), pl.BlockSpec(memory_space=pl.ANY)),
        scratch_shapes=[
            vmem((ROWS * 16, 128), F32),
            vmem((4, ROWS, 512), BF16), vmem((4, ROWS, 512), BF16),
            vmem((4, ROWS, W), F32), vmem((4, ROWS, W), F32),
            vmem((4, ROWS, 2 * W), BF16), vmem((4, ROWS, 2 * W), BF16),
            vmem((ROWS, W), F32), vmem((ROWS, W), F32), vmem((8, 64, W), F32),
            vmem((128, W), F32), vmem((W, W), F32), vmem((8, 16, W), F32),
            vmem((128, W), F32), vmem((W, W), F32), vmem((8, 16, W), F32),
            vmem((W, 2 * W), F32), vmem((2, ROWS, 2 * W), BF16),
            dma, dma((4,)),
        ] + gather_sems + gather_sems + small_sems + small_sems + [dma((2, 8)), dma((2, 8))],
        compiler_params=pltpu.CompilerParams(
            collective_id=0, has_side_effects=True, vmem_limit_bytes=56 * 2**20),
        cost_estimate=pl.CostEstimate(flops=5 * 10**9, bytes_accessed=9 * 2**20, transcendentals=0),
    )(panel.reshape(ROWS, W), matrix.reshape(ROWS * 16, 128))
    return factor, updated.reshape(matrix.shape)


def solution(mesh):
    in_specs = (P(None, "row", None), P(None, "row", None, "col"))
    out_specs = (P(), P(None, "row", None, "col"))
    return jax.shard_map(shards, mesh=mesh, in_specs=in_specs, out_specs=out_specs, check_vma=False)
```

time: 540 us -> 154 us (0.29)
  waiting for transfers between devices: 418 us -> 0 us
  Pallas kernels: 0 us -> 147 us
  other arithmetic: 60.9 us -> 0 us
  matrix products: 28.2 us -> 0 us
  between operations: 15.3 us -> 0.64 us
  local copies, waits for them, and re-layouts: 17 us -> 6.24 us
    psum x4 -> x0, waiting for transfers between devices: 418 us -> none  [the longest x1 122 us: shards(): gram = lax.psum(jnp.dot(rows.T, rows, precision=highest), 'row')]
    pallas_call x0 -> x1, Pallas kernels: none -> 147 us  [shards(): pl.pallas_call(body, out_shape=(jax.ShapeDtypeStruct((W, W), F32), jax.Sh...]
    another operation x9 -> x0, other arithmetic: 54.4 us -> none  [the longest x6 34 us: shards(): lower = jnp.linalg.cholesky(gram)]
    dot_general x5 -> x0, matrix products: 23.2 us -> none  [the longest x1 10.3 us: shards(): result = local - jnp.dot(left_side, right_side.T, precision=highest)]
  transfers between devices with their start and end apart: 4 -> 0, of which waited for: 4 -> 0; matrix products, arithmetic and copies ran while one was open for 1% -> 0% of each run, Pallas kernels for 0% -> 0%
where the time goes in v1:
time: 154 us
  Pallas kernels  147 us (95%)
  local copies, waits for them, and re-layouts  6.24 us (4%)
    pallas_call x1, Pallas kernels, shards(): pl.pallas_call(body, out_shape=(jax.ShapeDtypeStruct((W, W), F32), jax.Sh...  147 us
    unnamed x2, local copies, waits for them, and re-layouts  6.24 us

profile of v1, /device:TPU:1, one launch (start us, length us, event | category | flops | bytes accessed | tf_op | source)
XLA Modules:
  0.0 153.9 jit_solution(8011763164604298615)
XLA Ops:
  0.6 147.0 %shard_map.41 = (f32[256,256]{1,0:T(8,128)}, f32[8192,128]{1,0:T(8,128)}) custom-call(f32[512,256]{1,0:T(8,128)} %bitcast.5, f32[8192,128]{1,0:T(8,128)} %bitcast.4), custom_call_target="tpu_custom_call" | custom-call | flops 5000000000 | bytes 9437184 | tf_op jit(solution)/shard_map/pallas_call | solution.py:305
  147.6 1.7 %copy.6 = f32[256,256]{1,0:T(8,128)} copy(f32[256,256]{1,0:T(8,128)} %get-tuple-element.8) | data formatting | bytes 524288
  149.3 4.6 %copy.7 = f32[4,128,16,128]{3,2,1,0:T(8,128)} copy(f32[4,128,16,128]{3,2,1,0:T(8,128)} %bitcast.3) | data formatting | bytes 8388608

commit v2 on v0

v2 whole, which is shorter than its diff:
```python
import jax
import jax.numpy as jnp
from jax import lax
from jax.experimental import pallas as pl
from jax.experimental.pallas import tpu as pltpu
from jax.sharding import PartitionSpec as P

MESH = pl.DeviceIdType.MESH
HIGHEST = lax.Precision.HIGHEST
F32 = jnp.float32
BF16 = jnp.bfloat16
W = 256
H = 128
ROWS = 512
NB = 32

NN = (((1,), (0,)), ((), ()))
NT = (((1,), (1,)), ((), ()))
TN = (((0,), (0,)), ((), ()))


def remote(src, dst, send, recv, row, col):
    return pltpu.make_async_remote_copy(
        src_ref=src, dst_ref=dst, send_sem=send, recv_sem=recv,
        device_id={"row": row, "col": col}, device_id_type=MESH)


def split(x):
    hi = x.astype(BF16)
    return hi, (x - hi.astype(F32)).astype(BF16)


def dot(a, b, dims=NN, precision=None):
    return lax.dot_general(a, b, dims, precision=precision, preferred_element_type=F32)


def dot3(a, b, dims=NN):
    ah, al = split(a)
    bh, bl = split(b)
    return dot(ah, bh, dims) + (dot(ah, bl, dims) + dot(al, bh, dims))


def factorize(gram, work):
    lane = lax.broadcasted_iota(jnp.int32, (NB, 128), 1)
    sub = lax.broadcasted_iota(jnp.int32, (NB, 128), 0)
    eye = (lane == sub).astype(F32)
    for b in range(W // NB):
        lo = b * NB
        left = gram[lo:lo + NB, :]
        unit = (lax.broadcasted_iota(jnp.int32, (NB, W), 1) ==
                lax.broadcasted_iota(jnp.int32, (NB, W), 0) + lo).astype(F32)
        rows = jnp.concatenate([left, unit], axis=1)
        if b:
            rows = rows - dot(work[0:lo, lo:lo + NB], work[0:lo, :], TN, HIGHEST)
        tile = jnp.concatenate([rows[:, lo:lo + NB], eye[:, :NB], jnp.zeros((NB, 128 - 2 * NB), F32)], axis=1)
        for i in range(NB):
            row = tile[i:i + 1, :]
            factor = tile[:, i:i + 1] * (1.0 / tile[i:i + 1, i:i + 1])
            tile = jnp.where(sub > i, tile - factor * row, tile)
        pivots = jnp.sum(jnp.where(lane == sub, tile, 0.0), axis=1, keepdims=True)
        inverse = tile[:, NB:2 * NB] * lax.rsqrt(pivots)
        work[lo:lo + NB, :] = dot(inverse, rows, NN, HIGHEST)
        yield


def body(panel, a_hbm, factor_out, out_hbm,
         abuf, plh, yp, yq, rs, ytc, ptc, yz, yr, chi, clo, lhs,
         gpart, gpair, grs, gsum, spart, srs, szs, ssum, work,
         a_sem, o_sem, pair, rs_sem, ag_sem, sib_sem, z_sem, x_sem,
         px_send, px_recv, p0, py, psib, gp, gr, ga, gs, sr, sz, sa, ss):
    r = lax.axis_index("row")
    c = lax.axis_index("col")
    core = r % 2
    m = r // 2
    x = m % 4
    y = m // 4
    sib = r + 1 - 2 * core
    column = 2 * x + core
    source_x = c // 2
    source_core = c % 2
    on_source = x == source_x
    is_source = r % 8 == c
    is_second = jnp.logical_and(on_source, core != source_core)
    off_source = jnp.logical_not(on_source)
    mine = pl.ds(pl.multiple_of(core * H, H), H)
    other = pl.ds(pl.multiple_of(H - core * H, H), H)

    def in_plane(xx, yy, kk):
        return (yy * 4 + xx) * 2 + kk

    load = pltpu.make_async_copy(a_hbm, abuf, a_sem)
    load.start()

    barrier = pltpu.get_barrier_semaphore()

    def greet(row, col):
        pl.semaphore_signal(barrier, inc=1, device_id={"row": row, "col": col}, device_id_type=MESH)

    greet(sib, c)
    for d in range(1, 4):
        greet(in_plane((x + d) % 4, y, 1 - core), c)
    for p in range(1, 16):
        greet(((m + p) % 16) * 2 + core, c)
    for p in range(1, 8):
        greet(r, (c + p) % 8)

    flipped = panel[...].T
    high, low = split(flipped)
    plh[0:W, :] = high
    plh[W:, :] = low
    gpart[...] = dot(flipped, flipped, NT, HIGHEST)

    @pl.when(is_source)
    def _():
        for i in range(4):
            ptc[4 * y + i] = flipped[:, i * H:(i + 1) * H]

    pl.semaphore_wait(barrier, 26)

    def to_plane(src, dst, sems, p):
        return remote(src, dst, sems.at[0, p], sems.at[1, p], ((m + p) % 16) * 2 + core, c)

    def to_col(src, dst, sems, p):
        return remote(src, dst, sems.at[0, p], sems.at[1, p], r, (c + p) % 8)

    def to_sib(src, dst, sems, *at):
        return remote(src, dst, sems.at[(0, *at)], sems.at[(1, *at)], sib, c)

    def block(q):
        return pl.ds(4 * q, 4)

    gram_pair = to_sib(gpart.at[other, :], gpair, gp)
    gram_pair.start()

    own_half = ptc.at[block(y), mine, :]
    whole = ptc.at[block(y), :, :]

    def px_copy(d, k):
        ref = ptc.at[block(y), k * H:(k + 1) * H, :]
        return remote(ref, ref, px_send.at[d - 1, k], px_recv, in_plane((x + d) % 4, y, k), c)

    share_whole = to_sib(whole, whole, p0)
    share_half = to_sib(own_half, own_half, p0)

    @pl.when(is_source)
    def _():
        share_whole.start()
        for d in (2, 1, 3):
            for k in range(2):
                px_copy(d, k).start()

    def small_out(part, slots, sems):
        for p in range(1, 16):
            rows = pl.ds(pl.multiple_of(((m + p) % 16) * 8, 8), 8)
            yield to_plane(part.at[rows, :], slots.at[p], sems, p)

    def small_back(total, sems, arriving):
        for p in range(1, 16):
            at = (m + 16 - p) % 16 if arriving else m
            ref = total.at[pl.ds(pl.multiple_of(core * H + at * 8, 8), 8), :]
            yield to_plane(ref, ref, sems, p)

    def small_sum(part, slots):
        value = part[pl.ds(pl.multiple_of(m * 8, 8), 8), :]
        for p in range(1, 16):
            value = value + slots[p]
        return value

    own_rows = pl.ds(pl.multiple_of(core * H + m * 8, 8), 8)

    gram_pair.wait_recv()
    gpair[...] = gpair[...] + gpart[mine, :]
    for copy in small_out(gpair, grs, gr):
        copy.start()

    load.wait()
    for q in range(4):
        value = jnp.concatenate([abuf[pl.ds(4 * i + q, ROWS, stride=16), :] for i in range(4)], axis=1)
        ah, al = split(value)
        both = dot(plh[...], ah)
        value = both[0:W] + (both[W:] + dot(plh[0:W, :], al))
        for i in range(4):
            yp[4 * q + i] = value[:, i * H:(i + 1) * H]
        to_sib(yp.at[4 * q:4 * q + 4, other, :], yq.at[4 * q:4 * q + 4], pair, q).start()

    for copy in small_out(gpair, grs, gr):
        copy.wait_recv()
    gsum[own_rows, :] = small_sum(gpair, grs)
    for copy in small_back(gsum, ga, False):
        copy.start()

    def pair_copy(q):
        return to_sib(yp.at[4 * q:4 * q + 4, other, :], yq.at[4 * q:4 * q + 4], pair, q)

    for q in range(4):
        pair_copy(q).wait_recv()
        for i in range(4):
            yp[4 * q + i, mine, :] = yp[4 * q + i, mine, :] + yq[4 * q + i]

    def rs_copy(p):
        return to_plane(yp.at[(m + p) % 16, mine, :], rs.at[p], rs_sem, p)

    for p in range(1, 16):
        rs_copy(p).start()

    for copy in small_back(gsum, ga, True):
        copy.wait_recv()
    gram_share = to_sib(gsum.at[mine, :], gsum.at[mine, :], gs)
    gram_share.start()
    to_sib(gsum.at[other, :], gsum.at[other, :], gs).wait_recv()

    blocks = factorize(gsum, work)
    next(blocks)

    @pl.when(is_second)
    def _():
        share_whole.wait_recv()

    @pl.when(off_source)
    def _():
        remote(own_half, own_half, px_send.at[0, 0], px_recv, sib, c).wait_recv()
        share_half.start()

    next(blocks)

    @pl.when(off_source)
    def _():
        theirs = ptc.at[block(y), other, :]
        to_sib(theirs, theirs, p0).wait_recv()

    next(blocks)

    for p in range(1, 16):
        rs_copy(p).wait_recv()
    piece = yp[m, mine, :]
    for p in range(1, 16):
        piece = piece + rs[p]
    ytc[m, mine, :] = piece
    own = ytc.at[m, mine, :]

    spart[...] = dot3(piece, ptc[m], NT)
    for copy in small_out(spart, srs, sr):
        copy.start()

    def z_copy(p):
        return to_col(own, yz.at[p], z_sem, p)

    def ag_copy(p, arriving):
        at = (m + 16 - p) % 16 if arriving else m
        ref = ytc.at[at, mine, :]
        return to_plane(ref, ref, ag_sem, p)

    def py_copy(d, arriving):
        at = (y + 4 - d) % 4 if arriving else y
        ref = ptc.at[block(at), mine, :]
        return remote(ref, ref, py.at[0, d - 1], py.at[1, d - 1], in_plane(x, (y + d) % 4, core), c)

    for p in range(1, 8):
        z_copy(p).start()
    for p in range(1, 16):
        ag_copy(p, False).start()
    for d in range(1, 4):
        py_copy(d, False).start()

    def x_copy(p):
        place = (c + 8 - p) % 8
        src = own if p == 0 else yz.at[p]
        return remote(src, yr.at[x, mine, :], x_sem.at[0, p], x_sem.at[1, column],
                      in_plane(place // 2, y, place % 2), c)

    def x_start(p):
        at_home = (c + 8 - p) % 8 == column

        @pl.when(at_home)
        def _():
            yr[x, mine, :] = ytc[m, mine, :] if p == 0 else yz[p]

        @pl.when(jnp.logical_not(at_home))
        def _():
            x_copy(p).start()

    x_start(0)
    next(blocks)
    for copy in small_out(spart, srs, sr):
        copy.wait_recv()
    szs[0] = small_sum(spart, srs)
    for p in range(1, 8):
        to_col(szs.at[0], szs.at[p], sz, p).start()
    next(blocks)
    for p in range(1, 8):
        to_col(szs.at[0], szs.at[p], sz, p).wait_recv()
    value = szs[0]
    for p in range(1, 8):
        value = value + szs[p]
    ssum[own_rows, :] = value
    for copy in small_back(ssum, sa, False):
        copy.start()
    next(blocks)
    for p in range(1, 8):
        z_copy(p).wait_recv()
        x_start(p)
    next(blocks)
    for copy in small_back(ssum, sa, True):
        copy.wait_recv()
    cross_share = to_sib(ssum.at[mine, :], ssum.at[mine, :], ss)
    cross_share.start()
    next(blocks)

    upper = lax.broadcasted_iota(jnp.int32, (W, W), 1) >= lax.broadcasted_iota(jnp.int32, (W, W), 0)
    factor_out[...] = jnp.where(upper, work[:, :W], 0.0)
    inverse = work[:, W:]
    metric = dot(inverse, inverse, TN, HIGHEST)
    first = 2.0 * dot3(panel[...], metric)
    lhs[0:ROWS, :W], lhs[ROWS:, :W] = split(first)

    def piece_share(p, arriving):
        at = (m + 16 - p) % 16
        ref = ytc.at[at, other if arriving else mine, :]
        return to_sib(ref, ref, sib_sem, p)

    def block_share(d, arriving):
        ref = ptc.at[block((y + 4 - d) % 4), other if arriving else mine, :]
        return to_sib(ref, ref, psib, d - 1)

    piece_share(0, False).start()
    for p in range(1, 16):
        ag_copy(p, True).wait_recv()
        piece_share(p, False).start()
    for d in range(1, 4):
        py_copy(d, True).wait_recv()
        block_share(d, False).start()

    to_sib(ssum.at[other, :], ssum.at[other, :], ss).wait_recv()
    for u in range(8):
        @pl.when(column != u)
        def _():
            ref = yr.at[u // 2, (u % 2) * H:(u % 2 + 1) * H, :]
            remote(ref, ref, x_sem.at[0, 0], x_sem.at[1, u], sib, c).wait_recv()
    image = jnp.concatenate([yr[i].T for i in range(4)], axis=0)
    second = 2.0 * dot3(image - dot3(first, ssum[...]), metric)
    lhs[0:ROWS, W:], lhs[ROWS:, W:] = split(second)

    for p in range(16):
        piece_share(p, True).wait_recv()
    for d in range(1, 4):
        block_share(d, True).wait_recv()

    for q in range(4):
        for i in range(4):
            lanes = pl.ds(i * H, H)
            chi[q, 0:W, lanes], clo[q, 0:W, lanes] = split(ytc[4 * q + i])
            chi[q, W:, lanes], clo[q, W:, lanes] = split(ptc[4 * q + i])
    half = ROWS // 2
    for s in range(2):
        lh = lhs[s * half:(s + 1) * half, :]
        ll = lhs[ROWS + s * half:ROWS + (s + 1) * half, :]
        for q in range(4):
            value = dot(lh, chi[q]) + (dot(ll, chi[q]) + dot(lh, clo[q]))
            for i in range(4):
                at = pl.ds(s * half * 16 + 4 * i + q, half, stride=16)
                abuf[at, :] = abuf[at, :] - value[:, i * H:(i + 1) * H]
        rows = pl.ds(s * half * 16, half * 16)
        pltpu.make_async_copy(abuf.at[rows, :], out_hbm.at[rows, :], o_sem.at[s]).start()

    gram_pair.wait_send()
    gram_share.wait_send()
    cross_share.wait_send()

    @pl.when(is_source)
    def _():
        share_whole.wait_send()
        for d in range(1, 4):
            for k in range(2):
                px_copy(d, k).wait_send()

    @pl.when(off_source)
    def _():
        share_half.wait_send()

    for q in range(4):
        pair_copy(q).wait_send()
    for d in range(1, 4):
        py_copy(d, False).wait_send()
        block_share(d, False).wait_send()
    for p in range(16):
        piece_share(p, False).wait_send()
        if p:
            rs_copy(p).wait_send()
            ag_copy(p, False).wait_send()
    for copies in (small_out(gpair, grs, gr), small_back(gsum, ga, False),
                   small_out(spart, srs, sr), small_back(ssum, sa, False)):
        for copy in copies:
            copy.wait_send()
    for p in range(8):
        @pl.when((c + 8 - p) % 8 != column)
        def _():
            x_copy(p).wait_send()

        if p:
            z_copy(p).wait_send()
            to_col(szs.at[0], szs.at[p], sz, p).wait_send()
    for s in range(2):
        rows = pl.ds(s * half * 16, half * 16)
        pltpu.make_async_copy(abuf.at[rows, :], out_hbm.at[rows, :], o_sem.at[s]).wait()


def shards(panel, matrix):
    vmem = pltpu.VMEM
    dma = pltpu.SemaphoreType.DMA
    factor, updated = pl.pallas_call(
        body,
        out_shape=(jax.ShapeDtypeStruct((W, W), F32), jax.ShapeDtypeStruct((ROWS * 16, H), F32)),
        in_specs=[pl.BlockSpec(memory_space=pltpu.VMEM), pl.BlockSpec(memory_space=pl.ANY)],
        out_specs=(pl.BlockSpec(memory_space=pltpu.VMEM), pl.BlockSpec(memory_space=pl.ANY)),
        scratch_shapes=[
            vmem((ROWS * 16, H), F32), vmem((2 * W, ROWS), BF16),
            vmem((16, W, H), F32), vmem((16, H, H), F32), vmem((16, H, H), F32),
            vmem((16, W, H), F32), vmem((16, W, H), F32), vmem((8, H, H), F32), vmem((4, W, H), F32),
            vmem((4, 2 * W, ROWS), BF16), vmem((4, 2 * W, ROWS), BF16), vmem((2 * ROWS, 2 * W), BF16),
            vmem((W, W), F32), vmem((H, W), F32), vmem((16, 8, W), F32), vmem((W, W), F32),
            vmem((H, W), F32), vmem((16, 8, W), F32), vmem((8, 8, W), F32), vmem((W, W), F32),
            vmem((W, 2 * W), F32),
            dma, dma((2,)), dma((2, 4)), dma((2, 16)), dma((2, 16)), dma((2, 16)), dma((2, 8)), dma((2, 8)),
            dma((3, 2)), dma, dma((2,)), dma((2, 3)), dma((2, 3)),
            dma((2,)), dma((2, 16)), dma((2, 16)), dma((2,)),
            dma((2, 16)), dma((2, 8)), dma((2, 16)), dma((2,)),
        ],
        compiler_params=pltpu.CompilerParams(
            collective_id=0, has_side_effects=True, vmem_limit_bytes=56 * 2**20),
        cost_estimate=pl.CostEstimate(flops=5 * 10**9, bytes_accessed=9 * 2**20, transcendentals=0),
    )(panel.reshape(ROWS, W), matrix.reshape(ROWS * 16, H))
    return factor, updated.reshape(matrix.shape)


def solution(mesh):
    in_specs = (P(None, "row", None), P(None, "row", None, "col"))
    out_specs = (P(), P(None, "row", None, "col"))
    return jax.shard_map(shards, mesh=mesh, in_specs=in_specs, out_specs=out_specs, check_vma=False)
```

time: 540 us -> 103 us (0.19)
  waiting for transfers between devices: 418 us -> 0 us
  Pallas kernels: 0 us -> 95.6 us
  other arithmetic: 60.9 us -> 0 us
  matrix products: 28.2 us -> 0 us
  between operations: 15.3 us -> 0.64 us
  local copies, waits for them, and re-layouts: 17 us -> 6.24 us
    psum x4 -> x0, waiting for transfers between devices: 418 us -> none  [the longest x1 122 us: shards(): gram = lax.psum(jnp.dot(rows.T, rows, precision=highest), 'row')]
    pallas_call x0 -> x1, Pallas kernels: none -> 95.6 us  [shards(): pl.pallas_call(body, out_shape=(jax.ShapeDtypeStruct((W, W), F32), jax.Sh...]
    another operation x9 -> x0, other arithmetic: 54.4 us -> none  [the longest x6 34 us: shards(): lower = jnp.linalg.cholesky(gram)]
    dot_general x5 -> x0, matrix products: 23.2 us -> none  [the longest x1 10.3 us: shards(): result = local - jnp.dot(left_side, right_side.T, precision=highest)]
  transfers between devices with their start and end apart: 4 -> 0, of which waited for: 4 -> 0; matrix products, arithmetic and copies ran while one was open for 1% -> 0% of each run, Pallas kernels for 0% -> 0%
where the time goes in v2:
time: 103 us
  Pallas kernels  95.6 us (93%)
  local copies, waits for them, and re-layouts  6.24 us (6%)
    pallas_call x1, Pallas kernels, shards(): pl.pallas_call(body, out_shape=(jax.ShapeDtypeStruct((W, W), F32), jax.Sh...  95.6 us
    unnamed x2, local copies, waits for them, and re-layouts  6.24 us

profile of v2, /device:TPU:1, one launch (start us, length us, event | category | flops | bytes accessed | tf_op | source)
XLA Modules:
  0.0 102.5 jit_solution(4399131165406807395)
XLA Ops:
  0.6 95.6 %shard_map.41 = (f32[256,256]{1,0:T(8,128)}, f32[8192,128]{1,0:T(8,128)}) custom-call(f32[512,256]{1,0:T(8,128)} %bitcast.5, f32[8192,128]{1,0:T(8,128)} %bitcast.4), custom_call_target="tpu_custom_call" | custom-call | flops 5000000000 | bytes 9437184 | tf_op jit(solution)/shard_map/pallas_call | solution.py:410
  96.3 1.7 %copy.6 = f32[256,256]{1,0:T(8,128)} copy(f32[256,256]{1,0:T(8,128)} %get-tuple-element.8) | data formatting | bytes 524288
  97.9 4.6 %copy.7 = f32[4,128,16,128]{3,2,1,0:T(8,128)} copy(f32[4,128,16,128]{3,2,1,0:T(8,128)} %bitcast.3) | data formatting | bytes 8388608

commit v3 on v2

--- a/solution.py
+++ b/solution.py
@@ -40,34 +40,52 @@
     return dot(ah, bh, dims) + (dot(ah, bl, dims) + dot(al, bh, dims))
 
 
+def eliminate(tile):
+    sub = lax.broadcasted_iota(jnp.int32, (8, 128), 0)
+    groups = NB // 8
+    rows = [tile[8 * g:8 * g + 8] for g in range(groups)]
+    for g in range(groups):
+        cols = [[jnp.broadcast_to(rows[h][:, 8 * g + k:8 * g + k + 1], (8, 128)) for h in range(g, groups)]
+                for k in range(8)]
+        for j in range(8):
+            inverse = 1.0 / cols[j][0][j:j + 1]
+            scaled = rows[g][j:j + 1] * inverse
+            for k in range(j + 1, 8):
+                ratio = cols[k][0][j:j + 1] * inverse
+                cols[k] = [a - b * ratio for a, b in zip(cols[k], cols[j])]
+            rows[g] = jnp.where(sub > j, rows[g] - cols[j][0] * scaled, rows[g])
+            for h in range(g + 1, groups):
+                rows[h] = rows[h] - cols[j][h - g] * scaled
+    return jnp.concatenate(rows, axis=0)
+
+
 def factorize(gram, work):
     lane = lax.broadcasted_iota(jnp.int32, (NB, 128), 1)
     sub = lax.broadcasted_iota(jnp.int32, (NB, 128), 0)
     eye = (lane == sub).astype(F32)
+    work[...] = jnp.zeros_like(work)
     for b in range(W // NB):
         lo = b * NB
-        left = gram[lo:lo + NB, :]
-        unit = (lax.broadcasted_iota(jnp.int32, (NB, W), 1) ==
-                lax.broadcasted_iota(jnp.int32, (NB, W), 0) + lo).astype(F32)
-        rows = jnp.concatenate([left, unit], axis=1)
+        start = lo // 128 * 128
+        span = (lo + NB + 127) // 128 * 128
+        unit = (lax.broadcasted_iota(jnp.int32, (NB, span), 1) ==
+                lax.broadcasted_iota(jnp.int32, (NB, span), 0) + lo).astype(F32)
+        rows = jnp.concatenate([gram[lo:lo + NB, start:], unit], axis=1)
         if b:
-            rows = rows - dot(work[0:lo, lo:lo + NB], work[0:lo, :], TN, HIGHEST)
-        tile = jnp.concatenate([rows[:, lo:lo + NB], eye[:, :NB], jnp.zeros((NB, 128 - 2 * NB), F32)], axis=1)
-        for i in range(NB):
-            row = tile[i:i + 1, :]
-            factor = tile[:, i:i + 1] * (1.0 / tile[i:i + 1, i:i + 1])
-            tile = jnp.where(sub > i, tile - factor * row, tile)
+            rows = rows - dot(work[0:lo, lo:lo + NB], work[0:lo, start:W + span], TN, HIGHEST)
+        square = rows[:, lo - start:lo - start + NB]
+        tile = eliminate(jnp.concatenate([square, eye[:, :NB], jnp.zeros((NB, 128 - 2 * NB), F32)], axis=1))
         pivots = jnp.sum(jnp.where(lane == sub, tile, 0.0), axis=1, keepdims=True)
         inverse = tile[:, NB:2 * NB] * lax.rsqrt(pivots)
-        work[lo:lo + NB, :] = dot(inverse, rows, NN, HIGHEST)
+        work[lo:lo + NB, start:W + span] = dot(inverse, rows, NN, HIGHEST)
         yield
 
 
-def body(panel, a_hbm, factor_out, out_hbm,
+def body(panel, a_hbm, factor_out, updated,
          abuf, plh, yp, yq, rs, ytc, ptc, yz, yr, chi, clo, lhs,
-         gpart, gpair, grs, gsum, spart, srs, szs, ssum, work,
-         a_sem, o_sem, pair, rs_sem, ag_sem, sib_sem, z_sem, x_sem,
-         px_send, px_recv, p0, py, psib, gp, gr, ga, gs, sr, sz, sa, ss):
+         gpart, gpair, gps, gsum, spart, szs, sps, ssum, work,
+         a_sem, pair, rs_sem, ag_sem, sib_sem, z_sem, x_sem,
+         px_send, px_recv, p0, py, psib, gp, gr, ga, gs, sz, sr, sa, ss):
     r = lax.axis_index("row")
     c = lax.axis_index("col")
     core = r % 2
@@ -129,7 +147,7 @@
     def block(q):
         return pl.ds(4 * q, 4)
 
-    gram_pair = to_sib(gpart.at[other, :], gpair, gp)
+    gram_pair = to_sib(gpart.at[pl.ds(pl.multiple_of(H - core * H + c * 16, 16), 16), :], gpair, gp)
     gram_pair.start()
 
     own_half = ptc.at[block(y), mine, :]
@@ -149,98 +167,108 @@
             for k in range(2):
                 px_copy(d, k).start()
 
-    def small_out(part, slots, sems):
+    own_rows = pl.ds(pl.multiple_of(core * H + c * 16, 16), 16)
+
+    def spread_plane(slots, sems):
         for p in range(1, 16):
-            rows = pl.ds(pl.multiple_of(((m + p) % 16) * 8, 8), 8)
-            yield to_plane(part.at[rows, :], slots.at[p], sems, p)
-
-    def small_back(total, sems, arriving):
-        for p in range(1, 16):
-            at = (m + 16 - p) % 16 if arriving else m
-            ref = total.at[pl.ds(pl.multiple_of(core * H + at * 8, 8), 8), :]
-            yield to_plane(ref, ref, sems, p)
-
-    def small_sum(part, slots):
-        value = part[pl.ds(pl.multiple_of(m * 8, 8), 8), :]
-        for p in range(1, 16):
+            yield to_plane(slots.at[0], slots.at[p], sems, p)
+
+    def spread_col(total, sems, arriving):
+        for p in range(1, 8):
+            at = (c + 8 - p) % 8 if arriving else c
+            ref = total.at[pl.ds(pl.multiple_of(core * H + at * 16, 16), 16), :]
+            yield to_col(ref, ref, sems, p)
+
+    def sum_slots(slots, n):
+        value = slots[0]
+        for p in range(1, n):
             value = value + slots[p]
         return value
 
-    own_rows = pl.ds(pl.multiple_of(core * H + m * 8, 8), 8)
-
     gram_pair.wait_recv()
-    gpair[...] = gpair[...] + gpart[mine, :]
-    for copy in small_out(gpair, grs, gr):
+    gps[0] = gpair[...] + gpart[own_rows, :]
+    for copy in spread_plane(gps, gr):
         copy.start()
 
+    def pair_copy(s):
+        return to_sib(yp.at[block((y + s) % 4), other, :], yq.at[4 * s:4 * s + 4], pair, s)
+
+    def rs_copy(s, i):
+        target = 4 * ((y + s) % 4) + i
+        return remote(yp.at[target, mine, :], rs.at[m], rs_sem.at[0, 4 * s + i], rs_sem.at[1, m], target * 2 + core, c)
+
+    def scatter(s):
+        pair_copy(s).wait_recv()
+        for i in range(4):
+            at = 4 * ((y + s) % 4) + i
+            yp[at, mine, :] = yp[at, mine, :] + yq[4 * s + i]
+            if s:
+                rs_copy(s, i).start()
+            else:
+                @pl.when(x != i)
+                def _():
+                    rs_copy(s, i).start()
+
+                @pl.when(x == i)
+                def _():
+                    rs[m] = yp[m, mine, :]
+
     load.wait()
-    for q in range(4):
+    order = (2, 1, 3, 0)
+    for n, s in enumerate(order):
+        q = (y + s) % 4
         value = jnp.concatenate([abuf[pl.ds(4 * i + q, ROWS, stride=16), :] for i in range(4)], axis=1)
         ah, al = split(value)
         both = dot(plh[...], ah)
         value = both[0:W] + (both[W:] + dot(plh[0:W, :], al))
         for i in range(4):
             yp[4 * q + i] = value[:, i * H:(i + 1) * H]
-        to_sib(yp.at[4 * q:4 * q + 4, other, :], yq.at[4 * q:4 * q + 4], pair, q).start()
-
-    for copy in small_out(gpair, grs, gr):
+        pair_copy(s).start()
+        if n:
+            scatter(order[n - 1])
+    scatter(order[-1])
+
+    for copy in spread_plane(gps, gr):
         copy.wait_recv()
-    gsum[own_rows, :] = small_sum(gpair, grs)
-    for copy in small_back(gsum, ga, False):
+    gsum[own_rows, :] = sum_slots(gps, 16)
+    for copy in spread_col(gsum, ga, False):
         copy.start()
 
-    def pair_copy(q):
-        return to_sib(yp.at[4 * q:4 * q + 4, other, :], yq.at[4 * q:4 * q + 4], pair, q)
-
-    for q in range(4):
-        pair_copy(q).wait_recv()
-        for i in range(4):
-            yp[4 * q + i, mine, :] = yp[4 * q + i, mine, :] + yq[4 * q + i]
-
-    def rs_copy(p):
-        return to_plane(yp.at[(m + p) % 16, mine, :], rs.at[p], rs_sem, p)
-
-    for p in range(1, 16):
-        rs_copy(p).start()
-
-    for copy in small_back(gsum, ga, True):
+    @pl.when(is_second)
+    def _():
+        share_whole.wait_recv()
+
+    @pl.when(off_source)
+    def _():
+        remote(own_half, own_half, px_send.at[0, 0], px_recv, sib, c).wait_recv()
+        share_half.start()
+
+    for copy in spread_col(gsum, ga, True):
         copy.wait_recv()
     gram_share = to_sib(gsum.at[mine, :], gsum.at[mine, :], gs)
     gram_share.start()
     to_sib(gsum.at[other, :], gsum.at[other, :], gs).wait_recv()
 
-    blocks = factorize(gsum, work)
-    next(blocks)
-
-    @pl.when(is_second)
-    def _():
-        share_whole.wait_recv()
-
-    @pl.when(off_source)
-    def _():
-        remote(own_half, own_half, px_send.at[0, 0], px_recv, sib, c).wait_recv()
-        share_half.start()
-
-    next(blocks)
+    for u in range(16):
+        @pl.when(m != u)
+        def _():
+            remote(rs.at[u], rs.at[u], rs_sem.at[0, 0], rs_sem.at[1, u], sib, c).wait_recv()
+    piece = sum_slots(rs, 16)
+    ytc[m, mine, :] = piece
+    own = ytc.at[m, mine, :]
 
     @pl.when(off_source)
     def _():
         theirs = ptc.at[block(y), other, :]
         to_sib(theirs, theirs, p0).wait_recv()
 
-    next(blocks)
-
-    for p in range(1, 16):
-        rs_copy(p).wait_recv()
-    piece = yp[m, mine, :]
-    for p in range(1, 16):
-        piece = piece + rs[p]
-    ytc[m, mine, :] = piece
-    own = ytc.at[m, mine, :]
+    def cross_copy(p):
+        rows = pl.ds(pl.multiple_of((c + p) % 8 * 16, 16), 16)
+        return to_col(spart.at[rows, :], szs.at[p], sz, p)
 
     spart[...] = dot3(piece, ptc[m], NT)
-    for copy in small_out(spart, srs, sr):
-        copy.start()
+    for p in range(1, 8):
+        cross_copy(p).start()
 
     def z_copy(p):
         return to_col(own, yz.at[p], z_sem, p)
@@ -259,8 +287,6 @@
         z_copy(p).start()
     for p in range(1, 16):
         ag_copy(p, False).start()
-    for d in range(1, 4):
-        py_copy(d, False).start()
 
     def x_copy(p):
         place = (c + 8 - p) % 8
@@ -280,31 +306,27 @@
             x_copy(p).start()
 
     x_start(0)
-    next(blocks)
-    for copy in small_out(spart, srs, sr):
-        copy.wait_recv()
-    szs[0] = small_sum(spart, srs)
+    blocks = factorize(gsum, work)
+    for _ in range(4):
+        next(blocks)
+    szs[0] = spart[pl.ds(pl.multiple_of(c * 16, 16), 16), :]
     for p in range(1, 8):
-        to_col(szs.at[0], szs.at[p], sz, p).start()
-    next(blocks)
-    for p in range(1, 8):
-        to_col(szs.at[0], szs.at[p], sz, p).wait_recv()
-    value = szs[0]
-    for p in range(1, 8):
-        value = value + szs[p]
-    ssum[own_rows, :] = value
-    for copy in small_back(ssum, sa, False):
+        cross_copy(p).wait_recv()
+    sps[0] = sum_slots(szs, 8)
+    for copy in spread_plane(sps, sr):
         copy.start()
-    next(blocks)
+    for d in range(1, 4):
+        py_copy(d, False).start()
+    for _ in range(4):
+        next(blocks)
     for p in range(1, 8):
         z_copy(p).wait_recv()
         x_start(p)
-    next(blocks)
-    for copy in small_back(ssum, sa, True):
+    for copy in spread_plane(sps, sr):
         copy.wait_recv()
-    cross_share = to_sib(ssum.at[mine, :], ssum.at[mine, :], ss)
-    cross_share.start()
-    next(blocks)
+    ssum[own_rows, :] = sum_slots(sps, 16)
+    for copy in spread_col(ssum, sa, False):
+        copy.start()
 
     upper = lax.broadcasted_iota(jnp.int32, (W, W), 1) >= lax.broadcasted_iota(jnp.int32, (W, W), 0)
     factor_out[...] = jnp.where(upper, work[:, :W], 0.0)
@@ -326,6 +348,10 @@
     for p in range(1, 16):
         ag_copy(p, True).wait_recv()
         piece_share(p, False).start()
+    for copy in spread_col(ssum, sa, True):
+        copy.wait_recv()
+    cross_share = to_sib(ssum.at[mine, :], ssum.at[mine, :], ss)
+    cross_share.start()
     for d in range(1, 4):
         py_copy(d, True).wait_recv()
         block_share(d, False).start()
@@ -358,9 +384,7 @@
             value = dot(lh, chi[q]) + (dot(ll, chi[q]) + dot(lh, clo[q]))
             for i in range(4):
                 at = pl.ds(s * half * 16 + 4 * i + q, half, stride=16)
-                abuf[at, :] = abuf[at, :] - value[:, i * H:(i + 1) * H]
-        rows = pl.ds(s * half * 16, half * 16)
-        pltpu.make_async_copy(abuf.at[rows, :], out_hbm.at[rows, :], o_sem.at[s]).start()
+                updated[at, :] = abuf[at, :] - value[:, i * H:(i + 1) * H]
 
     gram_pair.wait_send()
     gram_share.wait_send()
@@ -377,18 +401,25 @@
     def _():
         share_half.wait_send()
 
-    for q in range(4):
-        pair_copy(q).wait_send()
+    for s in range(4):
+        pair_copy(s).wait_send()
+        for i in range(4):
+            if s:
+                rs_copy(s, i).wait_send()
+            else:
+                @pl.when(x != i)
+                def _():
+                    rs_copy(s, i).wait_send()
+
     for d in range(1, 4):
         py_copy(d, False).wait_send()
         block_share(d, False).wait_send()
     for p in range(16):
         piece_share(p, False).wait_send()
         if p:
-            rs_copy(p).wait_send()
             ag_copy(p, False).wait_send()
-    for copies in (small_out(gpair, grs, gr), small_back(gsum, ga, False),
-                   small_out(spart, srs, sr), small_back(ssum, sa, False)):
+    for copies in (spread_plane(gps, gr), spread_col(gsum, ga, False),
+                   spread_plane(sps, sr), spread_col(ssum, sa, False)):
         for copy in copies:
             copy.wait_send()
     for p in range(8):
@@ -398,38 +429,35 @@
 
         if p:
             z_copy(p).wait_send()
-            to_col(szs.at[0], szs.at[p], sz, p).wait_send()
-    for s in range(2):
-        rows = pl.ds(s * half * 16, half * 16)
-        pltpu.make_async_copy(abuf.at[rows, :], out_hbm.at[rows, :], o_sem.at[s]).wait()
+            cross_copy(p).wait_send()
 
 
 def shards(panel, matrix):
     vmem = pltpu.VMEM
     dma = pltpu.SemaphoreType.DMA
-    factor, updated = pl.pallas_call(
+    factor, result = pl.pallas_call(
         body,
-        out_shape=(jax.ShapeDtypeStruct((W, W), F32), jax.ShapeDtypeStruct((ROWS * 16, H), F32)),
-        in_specs=[pl.BlockSpec(memory_space=pltpu.VMEM), pl.BlockSpec(memory_space=pl.ANY)],
-        out_specs=(pl.BlockSpec(memory_space=pltpu.VMEM), pl.BlockSpec(memory_space=pl.ANY)),
+        out_shape=(pltpu.VMEM((W, W), F32), pltpu.VMEM((ROWS * 16, H), F32)),
+        in_specs=[pl.BlockSpec(memory_space=pltpu.VMEM), pl.BlockSpec(memory_space=pltpu.HBM)],
+        out_specs=(pl.BlockSpec(memory_space=pltpu.VMEM), pl.BlockSpec(memory_space=pltpu.VMEM)),
         scratch_shapes=[
             vmem((ROWS * 16, H), F32), vmem((2 * W, ROWS), BF16),
             vmem((16, W, H), F32), vmem((16, H, H), F32), vmem((16, H, H), F32),
             vmem((16, W, H), F32), vmem((16, W, H), F32), vmem((8, H, H), F32), vmem((4, W, H), F32),
             vmem((4, 2 * W, ROWS), BF16), vmem((4, 2 * W, ROWS), BF16), vmem((2 * ROWS, 2 * W), BF16),
-            vmem((W, W), F32), vmem((H, W), F32), vmem((16, 8, W), F32), vmem((W, W), F32),
-            vmem((H, W), F32), vmem((16, 8, W), F32), vmem((8, 8, W), F32), vmem((W, W), F32),
+            vmem((W, W), F32), vmem((16, W), F32), vmem((16, 16, W), F32), vmem((W, W), F32),
+            vmem((H, W), F32), vmem((8, 16, W), F32), vmem((16, 16, W), F32), vmem((W, W), F32),
             vmem((W, 2 * W), F32),
-            dma, dma((2,)), dma((2, 4)), dma((2, 16)), dma((2, 16)), dma((2, 16)), dma((2, 8)), dma((2, 8)),
+            dma, dma((2, 4)), dma((2, 16)), dma((2, 16)), dma((2, 16)), dma((2, 8)), dma((2, 8)),
             dma((3, 2)), dma, dma((2,)), dma((2, 3)), dma((2, 3)),
-            dma((2,)), dma((2, 16)), dma((2, 16)), dma((2,)),
-            dma((2, 16)), dma((2, 8)), dma((2, 16)), dma((2,)),
+            dma((2,)), dma((2, 16)), dma((2, 8)), dma((2,)),
+            dma((2, 8)), dma((2, 16)), dma((2, 8)), dma((2,)),
         ],
         compiler_params=pltpu.CompilerParams(
-            collective_id=0, has_side_effects=True, vmem_limit_bytes=56 * 2**20),
+            collective_id=0, has_side_effects=True, vmem_limit_bytes=54 * 2**20),
         cost_estimate=pl.CostEstimate(flops=5 * 10**9, bytes_accessed=9 * 2**20, transcendentals=0),
     )(panel.reshape(ROWS, W), matrix.reshape(ROWS * 16, H))
-    return factor, updated.reshape(matrix.shape)
+    return factor, result.reshape(matrix.shape)
 
 
 def solution(mesh):

time: 103 us -> 82.9 us (0.80)
  Pallas kernels: 95.6 us -> 79.4 us
  local copies, waits for them, and re-layouts: 6.24 us -> 2.72 us
    pallas_call x1, Pallas kernels: 95.6 us -> 79.4 us  [shards(): pl.pallas_call(body, out_shape=(pltpu.VMEM((W, W), F32), pltpu.VMEM((ROWS...]
    unnamed x2, local copies, waits for them, and re-layouts: 6.24 us -> 2.72 us
where the time goes in v3:
time: 82.9 us; the launch traced here: 82.8 us
  Pallas kernels  79.4 us (96%)
  local copies, waits for them, and re-layouts  2.72 us (3%)
    pallas_call x1, Pallas kernels, shards(): pl.pallas_call(body, out_shape=(pltpu.VMEM((W, W), F32), pltpu.VMEM((ROWS...  79.4 us
    unnamed x2, local copies, waits for them, and re-layouts  2.72 us

profile of v3, /device:TPU:1, one launch (start us, length us, event | category | flops | bytes accessed | tf_op | source)
XLA Modules:
  0.0 82.8 jit_solution(8264695616098870487)
XLA Ops:
  0.6 79.4 %shard_map.41 = (f32[256,256]{1,0:T(8,128)S(1)}, f32[8192,128]{1,0:T(8,128)S(1)}) custom-call(f32[512,256]{1,0:T(8,128)} %bitcast.5, f32[8192,128]{1,0:T(8,128)} %bitcast.4), custom_call_target="tpu_custom_call" | custom-call | flops 5000000000 | bytes 9437184 | tf_op jit(solution)/shard_map/pallas_call | solution.py:438
  80.0 0.7 copy.6
  80.7 2.0 %copy.7 = f32[4,128,16,128]{3,2,1,0:T(8,128)} copy(f32[4,128,16,128]{3,2,1,0:T(8,128)S(1)} %bitcast.3) | data formatting | bytes 8388608

commit v4 on v3

--- a/solution.py
+++ b/solution.py
@@ -243,12 +243,13 @@
         remote(own_half, own_half, px_send.at[0, 0], px_recv, sib, c).wait_recv()
         share_half.start()
 
-    for copy in spread_col(gsum, ga, True):
-        copy.wait_recv()
-    gram_share = to_sib(gsum.at[mine, :], gsum.at[mine, :], gs)
-    gram_share.start()
-    to_sib(gsum.at[other, :], gsum.at[other, :], gs).wait_recv()
-
+    def py_copy(d, arriving):
+        at = (y + 4 - d) % 4 if arriving else y
+        ref = ptc.at[block(at), mine, :]
+        return remote(ref, ref, py.at[0, d - 1], py.at[1, d - 1], in_plane(x, (y + d) % 4, core), c)
+
+    for d in range(1, 4):
+        py_copy(d, False).start()
     for u in range(16):
         @pl.when(m != u)
         def _():
@@ -278,11 +279,6 @@
         ref = ytc.at[at, mine, :]
         return to_plane(ref, ref, ag_sem, p)
 
-    def py_copy(d, arriving):
-        at = (y + 4 - d) % 4 if arriving else y
-        ref = ptc.at[block(at), mine, :]
-        return remote(ref, ref, py.at[0, d - 1], py.at[1, d - 1], in_plane(x, (y + d) % 4, core), c)
-
     for p in range(1, 8):
         z_copy(p).start()
     for p in range(1, 16):
@@ -306,6 +302,12 @@
             x_copy(p).start()
 
     x_start(0)
+    for copy in spread_col(gsum, ga, True):
+        copy.wait_recv()
+    gram_share = to_sib(gsum.at[mine, :], gsum.at[mine, :], gs)
+    gram_share.start()
+    to_sib(gsum.at[other, :], gsum.at[other, :], gs).wait_recv()
+
     blocks = factorize(gsum, work)
     for _ in range(4):
         next(blocks)
@@ -315,8 +317,6 @@
     sps[0] = sum_slots(szs, 8)
     for copy in spread_plane(sps, sr):
         copy.start()
-    for d in range(1, 4):
-        py_copy(d, False).start()
     for _ in range(4):
         next(blocks)
     for p in range(1, 8):
@@ -345,6 +345,9 @@
         return to_sib(ref, ref, psib, d - 1)
 
     piece_share(0, False).start()
+    for d in range(1, 4):
+        py_copy(d, True).wait_recv()
+        block_share(d, False).start()
     for p in range(1, 16):
         ag_copy(p, True).wait_recv()
         piece_share(p, False).start()
@@ -353,38 +356,33 @@
     cross_share = to_sib(ssum.at[mine, :], ssum.at[mine, :], ss)
     cross_share.start()
     for d in range(1, 4):
-        py_copy(d, True).wait_recv()
-        block_share(d, False).start()
-
-    to_sib(ssum.at[other, :], ssum.at[other, :], ss).wait_recv()
+        block_share(d, True).wait_recv()
+    for q in range(4):
+        for i in range(4):
+            lanes = pl.ds(i * H, H)
+            chi[q, W:, lanes], clo[q, W:, lanes] = split(ptc[4 * q + i])
     for u in range(8):
         @pl.when(column != u)
         def _():
             ref = yr.at[u // 2, (u % 2) * H:(u % 2 + 1) * H, :]
             remote(ref, ref, x_sem.at[0, 0], x_sem.at[1, u], sib, c).wait_recv()
     image = jnp.concatenate([yr[i].T for i in range(4)], axis=0)
+    for p in range(16):
+        piece_share(p, True).wait_recv()
+    for q in range(4):
+        for i in range(4):
+            lanes = pl.ds(i * H, H)
+            chi[q, 0:W, lanes], clo[q, 0:W, lanes] = split(ytc[4 * q + i])
+    to_sib(ssum.at[other, :], ssum.at[other, :], ss).wait_recv()
     second = 2.0 * dot3(image - dot3(first, ssum[...]), metric)
     lhs[0:ROWS, W:], lhs[ROWS:, W:] = split(second)
 
-    for p in range(16):
-        piece_share(p, True).wait_recv()
-    for d in range(1, 4):
-        block_share(d, True).wait_recv()
-
     for q in range(4):
-        for i in range(4):
-            lanes = pl.ds(i * H, H)
-            chi[q, 0:W, lanes], clo[q, 0:W, lanes] = split(ytc[4 * q + i])
-            chi[q, W:, lanes], clo[q, W:, lanes] = split(ptc[4 * q + i])
-    half = ROWS // 2
-    for s in range(2):
-        lh = lhs[s * half:(s + 1) * half, :]
-        ll = lhs[ROWS + s * half:ROWS + (s + 1) * half, :]
-        for q in range(4):
-            value = dot(lh, chi[q]) + (dot(ll, chi[q]) + dot(lh, clo[q]))
-            for i in range(4):
-                at = pl.ds(s * half * 16 + 4 * i + q, half, stride=16)
-                updated[at, :] = abuf[at, :] - value[:, i * H:(i + 1) * H]
+        both = dot(lhs[...], chi[q])
+        value = both[0:ROWS] + (both[ROWS:] + dot(lhs[0:ROWS, :], clo[q]))
+        for i in range(4):
+            at = pl.ds(4 * i + q, ROWS, stride=16)
+            updated[at, :] = abuf[at, :] - value[:, i * H:(i + 1) * H]
 
     gram_pair.wait_send()
     gram_share.wait_send()

time: 82.9 us -> 78.1 us (0.942)
  Pallas kernels: 79.4 us -> 74.6 us
    pallas_call x1, Pallas kernels: 79.4 us -> 74.6 us  [shards(): pl.pallas_call(body, out_shape=(pltpu.VMEM((W, W), F32), pltpu.VMEM((ROWS...]
where the time goes in v4:
time: 78.1 us; the launch traced here: 78 us
  Pallas kernels  74.6 us (96%)
  local copies, waits for them, and re-layouts  2.72 us (3%)
    pallas_call x1, Pallas kernels, shards(): pl.pallas_call(body, out_shape=(pltpu.VMEM((W, W), F32), pltpu.VMEM((ROWS...  74.6 us
    unnamed x2, local copies, waits for them, and re-layouts  2.72 us

profile of v4, /device:TPU:1, one launch (start us, length us, event | category | flops | bytes accessed | tf_op | source)
XLA Modules:
  0.0 78.0 jit_solution(17893962852285139294)
XLA Ops:
  0.6 74.6 %shard_map.41 = (f32[256,256]{1,0:T(8,128)S(1)}, f32[8192,128]{1,0:T(8,128)S(1)}) custom-call(f32[512,256]{1,0:T(8,128)} %bitcast.5, f32[8192,128]{1,0:T(8,128)} %bitcast.4), custom_call_target="tpu_custom_call" | custom-call | flops 5000000000 | bytes 9437184 | tf_op jit(solution)/shard_map/pallas_call | solution.py:436
  75.3 0.7 copy.6
  76.0 2.0 %copy.7 = f32[4,128,16,128]{3,2,1,0:T(8,128)} copy(f32[4,128,16,128]{3,2,1,0:T(8,128)S(1)} %bitcast.3) | data formatting | bytes 8388608

commit v5 on v4

--- a/solution.py
+++ b/solution.py
@@ -153,9 +153,8 @@
     own_half = ptc.at[block(y), mine, :]
     whole = ptc.at[block(y), :, :]
 
-    def px_copy(d, k):
-        ref = ptc.at[block(y), k * H:(k + 1) * H, :]
-        return remote(ref, ref, px_send.at[d - 1, k], px_recv, in_plane((x + d) % 4, y, k), c)
+    def px_copy(d):
+        return remote(own_half, own_half, px_send.at[d - 1], px_recv, in_plane((x + d) % 4, y, core), c)
 
     share_whole = to_sib(whole, whole, p0)
     share_half = to_sib(own_half, own_half, p0)
@@ -164,8 +163,7 @@
     def _():
         share_whole.start()
         for d in (2, 1, 3):
-            for k in range(2):
-                px_copy(d, k).start()
+            px_copy(d).start()
 
     own_rows = pl.ds(pl.multiple_of(core * H + c * 16, 16), 16)
 
@@ -184,6 +182,12 @@
         for p in range(1, n):
             value = value + slots[p]
         return value
+
+    @pl.when(is_second)
+    def _():
+        share_whole.wait_recv()
+        for d in (2, 1, 3):
+            px_copy(d).start()
 
     gram_pair.wait_recv()
     gps[0] = gpair[...] + gpart[own_rows, :]
@@ -234,13 +238,9 @@
     for copy in spread_col(gsum, ga, False):
         copy.start()
 
-    @pl.when(is_second)
-    def _():
-        share_whole.wait_recv()
-
     @pl.when(off_source)
     def _():
-        remote(own_half, own_half, px_send.at[0, 0], px_recv, sib, c).wait_recv()
+        px_copy(1).wait_recv()
         share_half.start()
 
     def py_copy(d, arriving):
@@ -391,9 +391,11 @@
     @pl.when(is_source)
     def _():
         share_whole.wait_send()
+
+    @pl.when(on_source)
+    def _():
         for d in range(1, 4):
-            for k in range(2):
-                px_copy(d, k).wait_send()
+            px_copy(d).wait_send()
 
     @pl.when(off_source)
     def _():
@@ -447,7 +449,7 @@
             vmem((H, W), F32), vmem((8, 16, W), F32), vmem((16, 16, W), F32), vmem((W, W), F32),
             vmem((W, 2 * W), F32),
             dma, dma((2, 4)), dma((2, 16)), dma((2, 16)), dma((2, 16)), dma((2, 8)), dma((2, 8)),
-            dma((3, 2)), dma, dma((2,)), dma((2, 3)), dma((2, 3)),
+            dma((3,)), dma, dma((2,)), dma((2, 3)), dma((2, 3)),
             dma((2,)), dma((2, 16)), dma((2, 8)), dma((2,)),
             dma((2, 8)), dma((2, 16)), dma((2, 8)), dma((2,)),
         ],

time: 78.1 us -> 76.2 us (0.976)
  Pallas kernels: 74.6 us -> 72.7 us
    pallas_call x1, Pallas kernels: 74.6 us -> 72.7 us  [shards(): pl.pallas_call(body, out_shape=(pltpu.VMEM((W, W), F32), pltpu.VMEM((ROWS...]
where the time goes in v5:
time: 76.2 us; the launch traced here: 76.1 us
  Pallas kernels  72.7 us (95%)
  local copies, waits for them, and re-layouts  2.72 us (4%)
    pallas_call x1, Pallas kernels, shards(): pl.pallas_call(body, out_shape=(pltpu.VMEM((W, W), F32), pltpu.VMEM((ROWS...  72.7 us
    unnamed x2, local copies, waits for them, and re-layouts  2.72 us

profile of v5, /device:TPU:1, one launch (start us, length us, event | category | flops | bytes accessed | tf_op | source)
XLA Modules:
  0.0 76.1 jit_solution(10025288177739777629)
XLA Ops:
  0.6 72.7 %shard_map.41 = (f32[256,256]{1,0:T(8,128)S(1)}, f32[8192,128]{1,0:T(8,128)S(1)}) custom-call(f32[512,256]{1,0:T(8,128)} %bitcast.5, f32[8192,128]{1,0:T(8,128)} %bitcast.4), custom_call_target="tpu_custom_call" | custom-call | flops 5000000000 | bytes 9437184 | tf_op jit(solution)/shard_map/pallas_call | solution.py:438
  73.4 0.7 copy.6
  74.1 2.0 %copy.7 = f32[4,128,16,128]{3,2,1,0:T(8,128)} copy(f32[4,128,16,128]{3,2,1,0:T(8,128)S(1)} %bitcast.3) | data formatting | bytes 8388608

commit v6 on v5

--- a/solution.py
+++ b/solution.py
@@ -232,24 +232,24 @@
             scatter(order[n - 1])
     scatter(order[-1])
 
+    @pl.when(off_source)
+    def _():
+        px_copy(1).wait_recv()
+        share_half.start()
+
+    def py_copy(d, arriving):
+        at = (y + 4 - d) % 4 if arriving else y
+        ref = ptc.at[block(at), mine, :]
+        return remote(ref, ref, py.at[0, d - 1], py.at[1, d - 1], in_plane(x, (y + d) % 4, core), c)
+
+    for d in range(1, 4):
+        py_copy(d, False).start()
+
     for copy in spread_plane(gps, gr):
         copy.wait_recv()
     gsum[own_rows, :] = sum_slots(gps, 16)
     for copy in spread_col(gsum, ga, False):
         copy.start()
-
-    @pl.when(off_source)
-    def _():
-        px_copy(1).wait_recv()
-        share_half.start()
-
-    def py_copy(d, arriving):
-        at = (y + 4 - d) % 4 if arriving else y
-        ref = ptc.at[block(at), mine, :]
-        return remote(ref, ref, py.at[0, d - 1], py.at[1, d - 1], in_plane(x, (y + d) % 4, core), c)
-
-    for d in range(1, 4):
-        py_copy(d, False).start()
     for u in range(16):
         @pl.when(m != u)
         def _():

time: 76.2 us -> 74.1 us (0.972)
  Pallas kernels: 72.7 us -> 70.6 us
    pallas_call x1, Pallas kernels: 72.7 us -> 70.6 us  [shards(): pl.pallas_call(body, out_shape=(pltpu.VMEM((W, W), F32), pltpu.VMEM((ROWS...]
where the time goes in v6:
time: 74.1 us; the launch traced here: 74 us
  Pallas kernels  70.6 us (95%)
  local copies, waits for them, and re-layouts  2.72 us (4%)
    pallas_call x1, Pallas kernels, shards(): pl.pallas_call(body, out_shape=(pltpu.VMEM((W, W), F32), pltpu.VMEM((ROWS...  70.6 us
    unnamed x2, local copies, waits for them, and re-layouts  2.72 us

profile of v6, /device:TPU:1, one launch (start us, length us, event | category | flops | bytes accessed | tf_op | source)
XLA Modules:
  0.0 74.0 jit_solution(1655590388532542112)
XLA Ops:
  0.6 70.6 %shard_map.41 = (f32[256,256]{1,0:T(8,128)S(1)}, f32[8192,128]{1,0:T(8,128)S(1)}) custom-call(f32[512,256]{1,0:T(8,128)} %bitcast.5, f32[8192,128]{1,0:T(8,128)} %bitcast.4), custom_call_target="tpu_custom_call" | custom-call | flops 5000000000 | bytes 9437184 | tf_op jit(solution)/shard_map/pallas_call | solution.py:438
  71.2 0.7 copy.6
  71.9 2.0 %copy.7 = f32[4,128,16,128]{3,2,1,0:T(8,128)} copy(f32[4,128,16,128]{3,2,1,0:T(8,128)S(1)} %bitcast.3) | data formatting | bytes 8388608
